TPU v7x, 256 devices: a whole 4x4x8 slice. The times are simulated.
256 devices in a mesh: gx: 8 (over x, z_lo), gy: 32 (over y, z_hi, core).
Axes of the slice: x: 4, y: 4, z: 8 (z_hi: 4, z_lo: 2; z = z_hi * 2 + z_lo), core: 2. Of those that a mesh axis runs over, the one named last changes fastest.
Arguments:
- embeddings: bfloat16 [262144, 1024], P(('gx', 'gy')), may hold values from -7 to 7
Outputs:
- log_density: float32 [262144], P(('gx', 'gy'))
All inputs are finite; a program needn't handle non-finite values.
Results may differ from a plain program's by a relative error of at most 0.0003.
Values may be sent and summed in bfloat16 or wider, within the bound.
No kernel may reach another device: no remote copies, remote signals or barrier semaphores. Data moves between devices by JAX's collectives and lax.ppermute only.
A program may use at most 64 MiB of HBM per device.

v0:
```python
import jax
import jax.numpy as jnp
from jax import lax
from jax.sharding import PartitionSpec as P

ROUNDS = 4
BAND = 64


def shifted(value, axis, steps):
    count = lax.axis_size(axis)
    pairs = [(source, (source + steps) % count) for source in range(count)]
    return lax.ppermute(value, axis, pairs)


def half_norms(block):
    values = block.astype(jnp.float32)
    return jnp.sum(values * values, axis=1) / (2.0 * BAND)


def kernel_block(left, left_half, right, right_half):
    inner = lax.dot_general(
        left, right, (((1,), (1,)), ((), ())), preferred_element_type=jnp.float32
    )
    return jnp.exp(inner / BAND - left_half[:, None] - right_half[None, :])


def body(embeddings):
    rows = embeddings.shape[0]
    mine_half = half_norms(embeddings)
    diagonal = lax.broadcasted_iota(jnp.int32, (rows, rows), 0) == lax.broadcasted_iota(
        jnp.int32, (rows, rows), 1
    )
    own = jnp.where(
        diagonal, jnp.float32(0.0), kernel_block(embeddings, mine_half, embeddings, mine_half)
    )
    total = jnp.sum(own, axis=1)
    visitor = embeddings
    for step in range(ROUNDS):
        step_x = step % 2
        step_y = step + 1
        visitor = embeddings
        if step_x != 0:
            visitor = shifted(visitor, "gx", -step_x)
        visitor = shifted(visitor, "gy", -step_y)
        block = kernel_block(embeddings, mine_half, visitor, half_norms(visitor))
        total = total + jnp.sum(block, axis=1)
        columns = jnp.sum(block, axis=0)
        back = shifted(columns, "gy", step_y)
        if step_x != 0:
            back = shifted(back, "gx", step_x)
        total = total + back
    return mine_half + jnp.log(total)


def solution(mesh):
    in_specs = (P(("gx", "gy"), None),)
    out_specs = P(("gx", "gy"))
    return jax.shard_map(body, mesh=mesh, in_specs=in_specs, out_specs=out_specs, check_vma=False)
```

profile of v0, /device:TPU:128, one launch (start us, length us, event | category | flops | bytes accessed | tf_op | source)
XLA Modules:
  0.0 386.9 jit_solution(13089703588412602328)
XLA Ops:
  0.0 0.0 copy-start
  0.0 3.2 collective-permute-start.2
  3.2 0.0 collective-permute-start
  3.2 0.0 collective-permute-start.6
  3.2 2.2 multiply_reduce_fusion.4
  5.4 88.3 %collective-permute-done.2 = bf16[1024,1024]{1,0:T(8,128)(2,1)S(1)} collective-permute-done((bf16[1024,1024]{1,0:T(8,128)(2,1)}, bf16[1024,1024]{1,0:T(8,128)(2,1)S(1)}, u32[]{:S(2)}, u32[]{:S(2)}) %collective-permute-start.2) | collective-permute-done | bytes 2097184 | tf_op jit(solution)/shard_map/ppermute | solution.py:13
  93.7 0.5 collective-permute-start.8
  94.2 7.0 %collective-permute-start.3 = (bf16[1024,1024]{1,0:T(8,128)(2,1)S(1)}, bf16[1024,1024]{1,0:T(8,128)(2,1)S(1)}, u32[]{:S(2)}, u32[]{:S(2)}) collective-permute-start(bf16[1024,1024]{1,0:T(8,128)(2,1)S(1)} %collective-permute-done.2), channel_id=1, source_target_pairs={{0,30},{1,31},{2,0},{3,1},{4,2},{5,3},{6,4},{7,5},{8,6},{9,7},{10,... | collective-permute-start | bytes 6291464 | tf_op jit(solution)/shard_map/ppermute | solution.py:13
  101.2 0.0 collective-permute-done
  101.2 0.5 multiply_reduce_fusion.3
  101.7 0.0 collective-permute-done.6
  101.7 0.5 multiply_reduce_fusion.1
  102.2 0.0 copy-done
  102.2 2.4 fusion.8
  104.6 2.4 fusion.10
  106.9 83.2 %collective-permute-done.8 = bf16[1024,1024]{1,0:T(8,128)(2,1)S(1)} collective-permute-done((bf16[1024,1024]{1,0:T(8,128)(2,1)S(1)}, bf16[1024,1024]{1,0:T(8,128)(2,1)S(1)}, u32[]{:S(2)}, u32[]{:S(2)}) %collective-permute-start.8) | collective-permute-done | bytes 2097184 | tf_op jit(solution)/shard_map/ppermute | solution.py:13
  190.1 0.5 multiply_reduce_fusion
  190.6 170.1 %collective-permute-done.3 = bf16[1024,1024]{1,0:T(8,128)(2,1)S(1)} collective-permute-done((bf16[1024,1024]{1,0:T(8,128)(2,1)S(1)}, bf16[1024,1024]{1,0:T(8,128)(2,1)S(1)}, u32[]{:S(2)}, u32[]{:S(2)}) %collective-permute-start.3) | collective-permute-done | bytes 2097184 | tf_op jit(solution)/shard_map/ppermute | solution.py:13
  360.7 0.5 multiply_reduce_fusion.2
  361.2 2.4 fusion.9
  363.6 6.3 %fusion.1 = (f32[1024]{0:T(1024)S(1)}, f32[1024]{0:T(1024)S(1)}, f32[1024]{0:T(1024)S(1)}, f32[1024]{0:T(1024)S(1)}, f32[1024]{0:T(1024)S(1)}, /*index=5*/f32[1024]{0:T(1024)S(1)}, f32[1024]{0:T(1024)S(1)}, f32[1024]{0:T(1024)S(1)}) fusion(f32[1024,1024]{0,1:T(8,128)S(1)} %fusion.8, f32[1024]{0:T(1024)S(1)} %broadcast_multiply_fusion.3, ...), kind=kOutput, calls=%fused_computation.12 | convolution fusion | flops 2168446976 | bytes 16830464 | tf_op jit(solution)/shard_map/dot_general | solution.py:22
  370.0 4.3 %collective-permute-start.9 = (f32[1024]{0:T(1024)S(1)}, f32[1024]{0:T(1024)S(1)}, u32[]{:S(2)}, u32[]{:S(2)}) collective-permute-start(f32[1024]{0:T(1024)S(1)} %get-tuple-element.15), channel_id=1, source_target_pairs={{0,4},{1,5},{2,6},{3,7},{4,8},{5,9},{6,10},{7,11},{8,12},{9,13},{1... | collective-permute-start | bytes 12296 | tf_op jit(solution)/shard_map/ppermute | solution.py:13
  374.3 2.8 collective-permute-start.4
  377.1 0.0 collective-permute-start.7
  377.1 1.6 collective-permute-start.1
  378.7 0.0 collective-permute-done.9
  378.7 1.9 collective-permute-start.10
  380.6 0.0 collective-permute-done.4
  380.6 1.1 collective-permute-start.5
  381.7 2.7 select_reduce_fusion
  384.4 0.0 collective-permute-done.7
  384.4 0.0 collective-permute-done.1
  384.4 0.0 collective-permute-done.10
  384.4 1.9 collective-permute-done.5
  386.3 0.6 log_add_fusion
  (5 shorter events, 0.0 us)
Async XLA Ops:
  0.0 102.2 %copy-start = (bf16[1024,1024]{1,0:T(8,128)(2,1)S(1)}, bf16[1024,1024]{1,0:T(8,128)(2,1)}, u32[]{:S(2)}) copy-start(bf16[1024,1024]{1,0:T(8,128)(2,1)} %param.1) | copy-start | bytes 6291460
  0.0 93.7 %collective-permute-start.2 = (bf16[1024,1024]{1,0:T(8,128)(2,1)}, bf16[1024,1024]{1,0:T(8,128)(2,1)S(1)}, u32[]{:S(2)}, u32[]{:S(2)}) collective-permute-start(bf16[1024,1024]{1,0:T(8,128)(2,1)} %param.1), channel_id=1, source_target_pairs={{0,224},{32,0},{64,32},{96,64},{128,96},{160,128},{192,160},{224,1... | collective-permute-start | bytes 6291464 | tf_op jit(solution)/shard_map/ppermute | solution.py:13
  3.2 98.0 %collective-permute-start = (bf16[1024,1024]{1,0:T(8,128)(2,1)}, bf16[1024,1024]{1,0:T(8,128)(2,1)S(1)}, u32[]{:S(2)}, u32[]{:S(2)}) collective-permute-start(bf16[1024,1024]{1,0:T(8,128)(2,1)} %param.1), channel_id=1, source_target_pairs={{0,31},{1,0},{2,1},{3,2},{4,3},{5,4},{6,5},{7,6},{8,7},{9,8},{10,9... | collective-permute-start | bytes 6291464 | tf_op jit(solution)/shard_map/ppermute | solution.py:13
  3.2 98.4 %collective-permute-start.6 = (bf16[1024,1024]{1,0:T(8,128)(2,1)}, bf16[1024,1024]{1,0:T(8,128)(2,1)S(1)}, u32[]{:S(2)}, u32[]{:S(2)}) collective-permute-start(bf16[1024,1024]{1,0:T(8,128)(2,1)} %param.1), channel_id=1, source_target_pairs={{0,29},{1,30},{2,31},{3,0},{4,1},{5,2},{6,3},{7,4},{8,5},{9,6},{10... | collective-permute-start | bytes 6291464 | tf_op jit(solution)/shard_map/ppermute | solution.py:13
  93.7 96.4 %collective-permute-start.8 = (bf16[1024,1024]{1,0:T(8,128)(2,1)S(1)}, bf16[1024,1024]{1,0:T(8,128)(2,1)S(1)}, u32[]{:S(2)}, u32[]{:S(2)}) collective-permute-start(bf16[1024,1024]{1,0:T(8,128)(2,1)S(1)} %collective-permute-done.2), channel_id=1, source_target_pairs={{0,28},{1,29},{2,30},{3,31},{4,0},{5,1},{6,2},{7,3},{8,4},{9,5},{1... | collective-permute-start | bytes 6291464 | tf_op jit(solution)/shard_map/ppermute | solution.py:13
  94.2 266.5 %collective-permute-start.3 = (bf16[1024,1024]{1,0:T(8,128)(2,1)S(1)}, bf16[1024,1024]{1,0:T(8,128)(2,1)S(1)}, u32[]{:S(2)}, u32[]{:S(2)}) collective-permute-start(bf16[1024,1024]{1,0:T(8,128)(2,1)S(1)} %collective-permute-done.2), channel_id=1, source_target_pairs={{0,30},{1,31},{2,0},{3,1},{4,2},{5,3},{6,4},{7,5},{8,6},{9,7},{10,... | collective-permute-start | bytes 6291464 | tf_op jit(solution)/shard_map/ppermute | solution.py:13
  370.0 8.8 %collective-permute-start.9 = (f32[1024]{0:T(1024)S(1)}, f32[1024]{0:T(1024)S(1)}, u32[]{:S(2)}, u32[]{:S(2)}) collective-permute-start(f32[1024]{0:T(1024)S(1)} %get-tuple-element.15), channel_id=1, source_target_pairs={{0,4},{1,5},{2,6},{3,7},{4,8},{5,9},{6,10},{7,11},{8,12},{9,13},{1... | collective-permute-start | bytes 12296 | tf_op jit(solution)/shard_map/ppermute | solution.py:13
  374.3 6.3 %collective-permute-start.4 = (f32[1024]{0:T(1024)S(1)}, f32[1024]{0:T(1024)S(1)}, u32[]{:S(2)}, u32[]{:S(2)}) collective-permute-start(f32[1024]{0:T(1024)S(1)} %get-tuple-element.17), channel_id=1, source_target_pairs={{0,2},{1,3},{2,4},{3,5},{4,6},{5,7},{6,8},{7,9},{8,10},{9,11},{10,... | collective-permute-start | bytes 12296 | tf_op jit(solution)/shard_map/ppermute | solution.py:13
  377.1 7.3 %collective-permute-start.7 = (f32[1024]{0:T(1024)S(1)}, f32[1024]{0:T(1024)S(1)}, u32[]{:S(2)}, u32[]{:S(2)}) collective-permute-start(f32[1024]{0:T(1024)S(1)} %get-tuple-element.13), channel_id=1, source_target_pairs={{0,3},{1,4},{2,5},{3,6},{4,7},{5,8},{6,9},{7,10},{8,11},{9,12},{10... | collective-permute-start | bytes 12296 | tf_op jit(solution)/shard_map/ppermute | solution.py:13
  377.1 7.3 %collective-permute-start.1 = (f32[1024]{0:T(1024)S(1)}, f32[1024]{0:T(1024)S(1)}, u32[]{:S(2)}, u32[]{:S(2)}) collective-permute-start(f32[1024]{0:T(1024)S(1)} %get-tuple-element.6), channel_id=1, source_target_pairs={{0,1},{1,2},{2,3},{3,4},{4,5},{5,6},{6,7},{7,8},{8,9},{9,10},{10,1... | collective-permute-start | bytes 12296 | tf_op jit(solution)/shard_map/ppermute | solution.py:13
  378.7 5.7 %collective-permute-start.10 = (f32[1024]{0:T(1024)S(1)}, f32[1024]{0:T(1024)S(1)}, u32[]{:S(2)}, u32[]{:S(2)}) collective-permute-start(f32[1024]{0:T(1024)S(1)} %collective-permute-done.9), channel_id=1, source_target_pairs={{0,32},{32,64},{64,96},{96,128},{128,160},{160,192},{192,224},{224... | collective-permute-start | bytes 12296 | tf_op jit(solution)/shard_map/ppermute | solution.py:13
  380.6 5.7 %collective-permute-start.5 = (f32[1024]{0:T(1024)S(1)}, f32[1024]{0:T(1024)S(1)}, u32[]{:S(2)}, u32[]{:S(2)}) collective-permute-start(f32[1024]{0:T(1024)S(1)} %collective-permute-done.4), channel_id=1, source_target_pairs={{0,32},{32,64},{64,96},{96,128},{128,160},{160,192},{192,224},{224... | collective-permute-start | bytes 12296 | tf_op jit(solution)/shard_map/ppermute | solution.py:13
where the time goes:
time: 393 us; the launch traced here: 387 us
  waiting for transfers between devices  344 us (88%)
  starting transfers between devices  22.4 us (6%)
  matrix products  16.2 us (4%)
  other arithmetic  4.7 us (1%)
    ppermute x11, waiting for transfers between devices, shifted(): return lax.ppermute(value, axis, pairs)  344 us
    ppermute x11, starting transfers between devices, shifted(): return lax.ppermute(value, axis, pairs)  22.4 us
    dot_general x5, matrix products, kernel_block(): lax.dot_general(left, right, (((1,), (1,)), ((), ())), preferred_element_...  16.2 us
  transfers between devices with their start and end apart: 11, of which 4 were waited for; matrix products, arithmetic and copies ran while one was open for 3% of the time, Pallas kernels for 0%

commit v1 on v0

v1 whole, which is shorter than its diff:
```python
import jax
import jax.numpy as jnp
from jax import lax
from jax.sharding import PartitionSpec as P

BAND = 64
AXES = ("gx", "gy")
NX, NY, NZ = 4, 4, 8

DEVICES = [
    (x, y, z, c) for x in range(NX) for y in range(NY) for z in range(NZ) for c in range(2)
]


def number(x, y, z, c):
    x, y, z = x % NX, y % NY, z % NZ
    return (2 * x + z % 2) * 32 + 8 * y + 2 * (z // 2) + c


def is_first(x, y, z, c):
    return c != z % 2


def hop_one(x, y, z, c):
    return (x, y, z + 1, c) if c else (x, y, z - 1, c)


def hop_two(x, y, z, c):
    if c:
        t = (z + 1) % NZ
        return (x, y - (t in (3, 5)) + (t == 0), t, c)
    t = (z - 1) % NZ
    return (x, y + (t in (0, 2, 4)), t, c)


def hop_three(x, y, z, c):
    return (x, y, z - 1, c) if c else (x, y + (z in (6, 7)), z + 1, c)


def own_across(x, y, z, c):
    if not is_first(x, y, z, c):
        return (x, y, z, 1 - c)
    return (x, y + 1, z, 0) if c else (x, y - (z in (1, 3, 5)), z, 1)


def own_along_x(x, y, z, c):
    if not is_first(x, y, z, c):
        return None
    return (x - 1, y - (z == 0), z, c) if c else (x + 1, y + (z == 7), z, c)


def two_along_x(x, y, z, c):
    if is_first(x, y, z, c):
        return None
    return (x + 1, y + 1, z, c) if c else (x - 1, y - 1, z, c)


def two_across(x, y, z, c):
    if not is_first(x, y, z, c):
        return None
    return (x, y + 1, z, 0) if c else (x, y - 1, z, 1)


def three_across(x, y, z, c):
    if is_first(x, y, z, c):
        return None
    return (x, y, z, 1 - c)


def route(*hops):
    pairs = []
    for source in DEVICES:
        at = source
        for hop in hops:
            at = at and hop(*at)
            at = at and (at[0] % NX, at[1] % NY, at[2] % NZ, at[3])
        if at:
            pairs.append((number(*source), number(*at)))
    return pairs


def back(pairs):
    return [(target, source) for source, target in pairs]


def move(value, pairs):
    return lax.ppermute(value, AXES, pairs)


def half_norms(block):
    values = block.astype(jnp.float32)
    return jnp.sum(values * values, axis=1) / (2.0 * BAND)


def kernel_block(left, left_half, right, right_half):
    inner = lax.dot_general(
        left, right, (((1,), (1,)), ((), ())), preferred_element_type=jnp.float32
    )
    return jnp.exp(inner / BAND - left_half[:, None] - right_half[None, :])


def sums(left, left_half, right, right_half):
    block = kernel_block(left, left_half, right, right_half)
    return jnp.sum(block, axis=1), jnp.sum(block, axis=0)


def body(own):
    rows = own.shape[0]
    first = lax.axis_index("gx") % 2 != lax.axis_index("gy") % 2

    def pick(a, b):
        return jnp.where(first, a, b)

    one = move(own, route(hop_one))
    across = move(own, route(own_across))
    along = move(own, route(own_along_x))
    own_late, _ = lax.optimization_barrier((own, one))
    two = move(one, route(hop_two))
    three = move(own_late, route(hop_three))
    two_c = move(two, route(two_across))
    two_x = move(two, route(two_along_x))
    three_c = move(three, route(three_across))

    own_half = half_norms(own)
    diagonal = lax.broadcasted_iota(jnp.int32, (rows, rows), 0) == lax.broadcasted_iota(
        jnp.int32, (rows, rows), 1
    )
    same = jnp.where(diagonal, jnp.float32(0.0), kernel_block(own, own_half, own, own_half))
    total = jnp.sum(same, axis=1)

    two_half = half_norms(two)
    b_left, b_right = sums(
        across, half_norms(across), pick(own, two), pick(own_half, two_half)
    )
    c_block, c_other = pick(along, two_c), pick(one, two)
    c_left, c_right = sums(c_block, half_norms(c_block), c_other, half_norms(c_other))
    three_half = half_norms(three)
    d_left, d_right = sums(three, three_half, two, two_half)
    e_block = pick(three_c, two_x)
    e_left, e_right = sums(e_block, half_norms(e_block), three, three_half)

    zero = jnp.zeros_like(total)
    total = total + pick(b_right, zero)
    total = total + move(b_left, back(route(own_across)))
    total = total + move(c_left, back(route(own_along_x)))
    one_pairs = [p for p in route(hop_one) if is_first(*PLACE[p[1]])]
    total = total + move(
        pick(c_right, c_left), back(one_pairs + route(hop_one, hop_two, two_across))
    )
    total = total + move(
        d_right + pick(zero, b_right + c_right), back(route(hop_one, hop_two))
    )
    total = total + move(d_left + e_right, back(route(hop_three)))
    total = total + move(
        e_left, back(route(hop_three, three_across) + route(hop_one, hop_two, two_along_x))
    )
    return own_half + jnp.log(total)


PLACE = {number(*device): device for device in DEVICES}


def solution(mesh):
    in_specs = (P(AXES, None),)
    return jax.shard_map(
        body, mesh=mesh, in_specs=in_specs, out_specs=P(AXES), check_vma=False
    )
```

time: 393 us -> 154 us (0.39)
  the two profiles are of different devices: /device:TPU:128 before, /device:TPU:6 now
where the time goes in v1:
time: 154 us
  waiting for transfers between devices  93.3 us (61%)
  starting transfers between devices  26.5 us (17%)
  matrix products  22 us (14%)
  other arithmetic  11.8 us (8%)
    ppermute x14, waiting for transfers between devices, move(): return lax.ppermute(value, AXES, pairs)  93.3 us
    ppermute x14, starting transfers between devices, move(): return lax.ppermute(value, AXES, pairs)  26.5 us
    dot_general x5, matrix products, kernel_block(): lax.dot_general(left, right, (((1,), (1,)), ((), ())), preferred_element_...  22 us
    reduce_sum x6, other arithmetic, half_norms(): return jnp.sum(values * values, axis=1) / (2.0 * BAND)  11.1 us
  transfers between devices with their start and end apart: 14, of which 6 were waited for; matrix products, arithmetic and copies ran while one was open for 22% of the time, Pallas kernels for 0%

profile of v1, /device:TPU:6, one launch (start us, length us, event | category | flops | bytes accessed | tf_op | source)
XLA Modules:
  0.0 153.8 jit_solution(1283304223021534092)
XLA Ops:
  0.0 5.9 %collective-permute-start = (bf16[1024,1024]{1,0:T(8,128)(2,1)}, bf16[1024,1024]{1,0:T(8,128)(2,1)}, u32[]{:S(2)}, u32[]{:S(2)}) collective-permute-start(bf16[1024,1024]{1,0:T(8,128)(2,1)} %param.1), channel_id=1, source_target_pairs={{0,38},{1,33},{32,0},{33,3},{2,32},{3,35},{34,2},{35,5},{4,34},{5,... | collective-permute-start | bytes 6291464 | tf_op jit(solution)/shard_map/ppermute | solution.py:87
  5.9 0.0 collective-permute-start.2
  5.9 23.9 %collective-permute-done = bf16[1024,1024]{1,0:T(8,128)(2,1)} collective-permute-done((bf16[1024,1024]{1,0:T(8,128)(2,1)}, bf16[1024,1024]{1,0:T(8,128)(2,1)}, u32[]{:S(2)}, u32[]{:S(2)}) %collective-permute-start) | collective-permute-done | bytes 2097184 | tf_op jit(solution)/shard_map/ppermute | solution.py:87
  29.7 3.7 %collective-permute-start.1 = (bf16[1024,1024]{1,0:T(8,128)(2,1)}, bf16[1024,1024]{1,0:T(8,128)(2,1)}, u32[]{:S(2)}, u32[]{:S(2)}) collective-permute-start(bf16[1024,1024]{1,0:T(8,128)(2,1)} %collective-permute-done), channel_id=1, source_target_pairs={{0,38},{1,33},{32,8},{33,3},{2,32},{3,59},{34,10},{35,5},{4,34},{5... | collective-permute-start | bytes 6291464 | tf_op jit(solution)/shard_map/ppermute | solution.py:87
  33.4 0.0 collective-permute-start.8
  33.4 0.8 collective-permute-start.4
  34.2 2.1 %multiply_reduce_fusion.6 = f32[1024]{0:T(1024)S(1)} fusion(bf16[1024,1024]{1,0:T(8,128)(2,1)} %param.1), kind=kLoop, calls=%fused_computation.12 | loop fusion | flops 3144704 | bytes 2101248 | tf_op jit(solution)/shard_map/reduce_sum | solution.py:92
  36.3 0.0 collective-permute-done.2
  36.3 2.1 %multiply_reduce_fusion.5 = f32[1024]{0:T(1024)S(1)} fusion(bf16[1024,1024]{1,0:T(8,128)(2,1)} %collective-permute-done.2), kind=kLoop, calls=%fused_computation.9 | loop fusion | flops 3144704 | bytes 2101248 | tf_op jit(solution)/shard_map/reduce_sum | solution.py:92
  38.4 0.0 copy-start
  38.4 54.2 %collective-permute-done.1 = bf16[1024,1024]{1,0:T(8,128)(2,1)} collective-permute-done((bf16[1024,1024]{1,0:T(8,128)(2,1)}, bf16[1024,1024]{1,0:T(8,128)(2,1)}, u32[]{:S(2)}, u32[]{:S(2)}) %collective-permute-start.1) | collective-permute-done | bytes 2097184 | tf_op jit(solution)/shard_map/ppermute | solution.py:87
  92.6 1.3 collective-permute-start.5
  93.9 3.4 %multiply_reduce_fusion.2 = (f32[1024]{0:T(1024)S(1)}, f32[1024]{0:T(1024)S(1)}) fusion(bf16[1024,1024]{1,0:T(8,128)(2,1)} %collective-permute-done, bf16[1024,1024]{1,0:T(8,128)(2,1)} %collective-permute-done.1, pred[]{:T(512)S(6)} %ne.15), kind=kLoop, calls=%fused_computation.5 | loop fusion | flops 7337984 | bytes 4202497 | tf_op jit(solution)/shard_map/reduce_sum | solution.py:92
  97.3 4.0 %collective-permute-start.11 = (bf16[1024,1024]{1,0:T(8,128)(2,1)}, bf16[1024,1024]{1,0:T(8,128)(2,1)S(1)}, u32[]{:S(2)}, u32[]{:S(2)}) collective-permute-start(bf16[1024,1024]{1,0:T(8,128)(2,1)} %collective-permute-done.1), channel_id=1, source_target_pairs={{0,216},{33,105},{2,218},{35,107},{4,220},{37,109},{6,222},{39,111... | collective-permute-start | bytes 6291464 | tf_op jit(solution)/shard_map/ppermute | solution.py:87
  101.3 1.9 %collective-permute-done.8 = bf16[1024,1024]{1,0:T(8,128)(2,1)} collective-permute-done((bf16[1024,1024]{1,0:T(8,128)(2,1)}, bf16[1024,1024]{1,0:T(8,128)(2,1)}, u32[]{:S(2)}, u32[]{:S(2)}) %collective-permute-start.8) | collective-permute-done | bytes 2097184 | tf_op jit(solution)/shard_map/ppermute | solution.py:87
  103.1 4.2 %collective-permute-start.10 = (bf16[1024,1024]{1,0:T(8,128)(2,1)}, bf16[1024,1024]{1,0:T(8,128)(2,1)S(1)}, u32[]{:S(2)}, u32[]{:S(2)}) collective-permute-start(bf16[1024,1024]{1,0:T(8,128)(2,1)} %collective-permute-done.8), channel_id=1, source_target_pairs={{0,1},{33,32},{2,3},{35,34},{4,5},{37,36},{6,7},{39,38},{8,9},{41,... | collective-permute-start | bytes 6291464 | tf_op jit(solution)/shard_map/ppermute | solution.py:87
  107.3 0.0 copy-done
  107.3 5.1 %fusion = (f32[1024]{0:T(1024)S(1)}, f32[1024]{0:T(1024)S(1)}) fusion(f32[1024]{0:T(1024)S(1)} %get-tuple-element.20, f32[1024]{0:T(1024)S(1)} %broadcast_multiply_fusion.5, bf16[1024,1024]{1,0:T(8,128)(2,1)} %collective-permute-done.2, bf16[1024,1024]{1,0:T(8,128)(2,1)S(1)} %copy-done, bf16[1024,1024]{1,0:T(8,128)(2,1)} %collective-permute-done.1, pred[]{:T(512)S(6)} %ne.15), kind=kOutput, calls=%fused_computation.13 | convolution fusion | flops 2153773056 | bytes 6307841 | tf_op jit(solution)/shard_map/dot_general | solution.py:96
  112.4 0.3 collective-permute-start.3
  112.7 2.1 %multiply_reduce_fusion.1 = f32[1024]{0:T(1024)S(1)} fusion(bf16[1024,1024]{1,0:T(8,128)(2,1)} %collective-permute-done.8), kind=kLoop, calls=%fused_computation.3 | loop fusion | flops 3144704 | bytes 2101248 | tf_op jit(solution)/shard_map/reduce_sum | solution.py:92
  114.8 4.6 %fusion.13 = f32[1024,1024]{0,1:T(8,128)S(1)} fusion(bf16[1024,1024]{1,0:T(8,128)(2,1)} %collective-permute-done.8, bf16[1024,1024]{1,0:T(8,128)(2,1)} %collective-permute-done.1), kind=kOutput, calls=%fused_computation.40 | convolution fusion | flops 2147483648 | bytes 8388608 | tf_op jit(solution)/shard_map/dot_general | solution.py:96
  119.4 0.0 collective-permute-done.4
  119.4 6.1 %collective-permute-done.5 = bf16[1024,1024]{1,0:T(8,128)(2,1)S(1)} collective-permute-done((bf16[1024,1024]{1,0:T(8,128)(2,1)}, bf16[1024,1024]{1,0:T(8,128)(2,1)S(1)}, u32[]{:S(2)}, u32[]{:S(2)}) %collective-permute-start.5) | collective-permute-done | bytes 2097184 | tf_op jit(solution)/shard_map/ppermute | solution.py:87
  125.5 0.8 multiply_reduce_fusion.3
  126.2 1.3 collective-permute-done.11
  127.5 0.0 collective-permute-done.10
  127.6 0.7 multiply_reduce_fusion
  128.3 4.5 %fusion.3 = (f32[1024]{0:T(1024)S(1)}, f32[1024]{0:T(1024)S(1)}) fusion(f32[1024]{0:T(1024)S(1)} %broadcast_multiply_fusion.2, f32[1024]{0:T(1024)S(1)} %broadcast_multiply_fusion.3, bf16[1024,1024]{1,0:T(8,128)(2,1)} %collective-permute-done, bf16[1024,1024]{1,0:T(8,128)(2,1)} %collective-permute-done.1, pred[]{:T(512)S(6)} %ne.15, ...), kind=kOutput, calls=%fused_computation.16 | convolution fusion | flops 2154821632 | bytes 8404993 | tf_op jit(solution)/shard_map/dot_general | solution.py:96
  132.8 0.7 collective-permute-start.6
  133.4 5.1 %fusion.5 = (f32[1024]{0:T(1024)S(1)}, f32[1024]{0:T(1024)S(1)}, f32[1024]{0:T(1024)S(1)}, f32[1024]{0:T(1024)S(1)}) fusion(f32[1024,1024]{0,1:T(8,128)S(1)} %fusion.13, f32[1024]{0:T(1024)S(1)} %get-tuple-element.21, f32[1024]{0:T(1024)S(1)} %broadcast_multiply_fusion.1, f32[1024]{0:T(1024)S(1)} %broadcast_multiply_fusion, ...), kind=kOutput, calls=%fused_computation.18 | convolution fusion | flops 2159013888 | bytes 10514433 | tf_op jit(solution)/shard_map/dot_general | solution.py:96
  138.6 0.1 collective-permute-start.7
  138.7 2.8 %collective-permute-start.9 = (f32[1024]{0:T(1024)S(1)}, f32[1024]{0:T(1024)S(1)}, u32[]{:S(2)}, u32[]{:S(2)}) collective-permute-start(f32[1024]{0:T(1024)S(1)} %get-tuple-element.23), channel_id=1, source_target_pairs={{6,0},{3,1},{38,32},{59,33},{8,2},{5,3},{32,34},{61,35},{10,4},{7,... | collective-permute-start | bytes 12296 | tf_op jit(solution)/shard_map/ppermute | solution.py:87
  141.5 3.0 %collective-permute-start.12 = (f32[1024]{0:T(1024)S(1)}, f32[1024]{0:T(1024)S(1)}, u32[]{:S(2)}, u32[]{:S(2)}) collective-permute-start(f32[1024]{0:T(1024)S(1)} %add.49), channel_id=1, source_target_pairs={{32,0},{39,1},{2,32},{1,33},{34,2},{33,3},{4,34},{3,35},{36,4},{35... | collective-permute-start | bytes 12296 | tf_op jit(solution)/shard_map/ppermute | solution.py:87
  144.4 0.0 collective-permute-done.3
  144.4 0.0 collective-permute-start.13
  144.4 2.7 %select_reduce_fusion = f32[1024]{0:T(1024)S(1)} fusion(bf16[1024,1024]{1,0:T(8,128)(2,1)S(1)} %copy-done, f32[1024]{0:T(1024)S(1)} %get-tuple-element.19), kind=kOutput, calls=%fused_computation.10 | convolution fusion | flops 2153774080 | bytes 2105344 | tf_op jit(solution)/shard_map/dot_general | solution.py:96
  147.1 0.0 collective-permute-done.7
  147.2 0.0 collective-permute-done.9
  147.2 0.0 collective-permute-done.6
  147.2 0.0 collective-permute-done.12
  147.2 6.0 %collective-permute-done.13 = f32[1024]{0:T(1024)S(1)} collective-permute-done((f32[1024]{0:T(1024)S(1)}, f32[1024]{0:T(1024)S(1)}, u32[]{:S(2)}, u32[]{:S(2)}) %collective-permute-start.13) | collective-permute-done | bytes 4128 | tf_op jit(solution)/shard_map/ppermute | solution.py:87
  153.2 0.6 log_add_fusion
  (8 shorter events, 0.0 us)
Async XLA Ops:
  0.0 29.7 %collective-permute-start = (bf16[1024,1024]{1,0:T(8,128)(2,1)}, bf16[1024,1024]{1,0:T(8,128)(2,1)}, u32[]{:S(2)}, u32[]{:S(2)}) collective-permute-start(bf16[1024,1024]{1,0:T(8,128)(2,1)} %param.1), channel_id=1, source_target_pairs={{0,38},{1,33},{32,0},{33,3},{2,32},{3,35},{34,2},{35,5},{4,34},{5,... | collective-permute-start | bytes 6291464 | tf_op jit(solution)/shard_map/ppermute | solution.py:87
  5.9 30.4 %collective-permute-start.2 = (bf16[1024,1024]{1,0:T(8,128)(2,1)}, bf16[1024,1024]{1,0:T(8,128)(2,1)}, u32[]{:S(2)}, u32[]{:S(2)}) collective-permute-start(bf16[1024,1024]{1,0:T(8,128)(2,1)} %param.1), channel_id=1, source_target_pairs={{0,1},{1,8},{32,57},{33,32},{2,3},{3,10},{34,59},{35,34},{4,5},{5,... | collective-permute-start | bytes 6291464 | tf_op jit(solution)/shard_map/ppermute | solution.py:87
  29.7 62.8 %collective-permute-start.1 = (bf16[1024,1024]{1,0:T(8,128)(2,1)}, bf16[1024,1024]{1,0:T(8,128)(2,1)}, u32[]{:S(2)}, u32[]{:S(2)}) collective-permute-start(bf16[1024,1024]{1,0:T(8,128)(2,1)} %collective-permute-done), channel_id=1, source_target_pairs={{0,38},{1,33},{32,8},{33,3},{2,32},{3,59},{34,10},{35,5},{4,34},{5... | collective-permute-start | bytes 6291464 | tf_op jit(solution)/shard_map/ppermute | solution.py:87
  33.4 69.7 %collective-permute-start.8 = (bf16[1024,1024]{1,0:T(8,128)(2,1)}, bf16[1024,1024]{1,0:T(8,128)(2,1)}, u32[]{:S(2)}, u32[]{:S(2)}) collective-permute-start(bf16[1024,1024]{1,0:T(8,128)(2,1)} %param.1), channel_id=1, source_target_pairs={{0,32},{1,39},{32,2},{33,1},{2,34},{3,33},{34,4},{35,3},{4,36},{5,... | collective-permute-start | bytes 6291464 | tf_op jit(solution)/shard_map/ppermute | solution.py:87
  33.4 86.0 %collective-permute-start.4 = (bf16[1024,1024]{1,0:T(8,128)(2,1)}, bf16[1024,1024]{1,0:T(8,128)(2,1)S(1)}, u32[]{:S(2)}, u32[]{:S(2)}) collective-permute-start(bf16[1024,1024]{1,0:T(8,128)(2,1)} %param.1), channel_id=1, source_target_pairs={{1,217},{32,96},{3,195},{34,98},{5,197},{36,100},{7,199},{38,110},... | collective-permute-start | bytes 6291464 | tf_op jit(solution)/shard_map/ppermute | solution.py:87
  38.4 68.9 %copy-start = (bf16[1024,1024]{1,0:T(8,128)(2,1)S(1)}, bf16[1024,1024]{1,0:T(8,128)(2,1)}, u32[]{:S(2)}) copy-start(bf16[1024,1024]{1,0:T(8,128)(2,1)} %param.1) | copy-start | bytes 6291460
  92.6 32.9 %collective-permute-start.5 = (bf16[1024,1024]{1,0:T(8,128)(2,1)}, bf16[1024,1024]{1,0:T(8,128)(2,1)S(1)}, u32[]{:S(2)}, u32[]{:S(2)}) collective-permute-start(bf16[1024,1024]{1,0:T(8,128)(2,1)} %collective-permute-done.1), channel_id=1, source_target_pairs={{1,8},{32,57},{3,10},{34,59},{5,12},{36,61},{7,14},{38,63},{9,16},... | collective-permute-start | bytes 6291464 | tf_op jit(solution)/shard_map/ppermute | solution.py:87
  97.3 30.3 %collective-permute-start.11 = (bf16[1024,1024]{1,0:T(8,128)(2,1)}, bf16[1024,1024]{1,0:T(8,128)(2,1)S(1)}, u32[]{:S(2)}, u32[]{:S(2)}) collective-permute-start(bf16[1024,1024]{1,0:T(8,128)(2,1)} %collective-permute-done.1), channel_id=1, source_target_pairs={{0,216},{33,105},{2,218},{35,107},{4,220},{37,109},{6,222},{39,111... | collective-permute-start | bytes 6291464 | tf_op jit(solution)/shard_map/ppermute | solution.py:87
  103.1 24.4 %collective-permute-start.10 = (bf16[1024,1024]{1,0:T(8,128)(2,1)}, bf16[1024,1024]{1,0:T(8,128)(2,1)S(1)}, u32[]{:S(2)}, u32[]{:S(2)}) collective-permute-start(bf16[1024,1024]{1,0:T(8,128)(2,1)} %collective-permute-done.8), channel_id=1, source_target_pairs={{0,1},{33,32},{2,3},{35,34},{4,5},{37,36},{6,7},{39,38},{8,9},{41,... | collective-permute-start | bytes 6291464 | tf_op jit(solution)/shard_map/ppermute | solution.py:87
  112.4 32.0 %collective-permute-start.3 = (f32[1024]{0:T(1024)S(1)}, f32[1024]{0:T(1024)S(1)}, u32[]{:S(2)}, u32[]{:S(2)}) collective-permute-start(f32[1024]{0:T(1024)S(1)} %get-tuple-element.7), channel_id=1, source_target_pairs={{1,0},{8,1},{57,32},{32,33},{3,2},{10,3},{59,34},{34,35},{5,4},{12... | collective-permute-start | bytes 12296 | tf_op jit(solution)/shard_map/ppermute | solution.py:87
  132.8 14.4 %collective-permute-start.6 = (f32[1024]{0:T(1024)S(1)}, f32[1024]{0:T(1024)S(1)}, u32[]{:S(2)}, u32[]{:S(2)}) collective-permute-start(f32[1024]{0:T(1024)S(1)} %get-tuple-element.9), channel_id=1, source_target_pairs={{217,1},{96,32},{195,3},{98,34},{197,5},{100,36},{199,7},{110,38},... | collective-permute-start | bytes 12296 | tf_op jit(solution)/shard_map/ppermute | solution.py:87
  138.6 8.5 %collective-permute-start.7 = (f32[1024]{0:T(1024)S(1)}, f32[1024]{0:T(1024)S(1)}, u32[]{:S(2)}, u32[]{:S(2)}) collective-permute-start(f32[1024]{0:T(1024)S(1)} %get-tuple-element.22), channel_id=1, source_target_pairs={{38,0},{3,33},{32,2},{5,35},{34,4},{7,37},{36,6},{1,39},{46,8},{11... | collective-permute-start | bytes 12296 | tf_op jit(solution)/shard_map/ppermute | solution.py:87
  138.7 8.5 %collective-permute-start.9 = (f32[1024]{0:T(1024)S(1)}, f32[1024]{0:T(1024)S(1)}, u32[]{:S(2)}, u32[]{:S(2)}) collective-permute-start(f32[1024]{0:T(1024)S(1)} %get-tuple-element.23), channel_id=1, source_target_pairs={{6,0},{3,1},{38,32},{59,33},{8,2},{5,3},{32,34},{61,35},{10,4},{7,... | collective-permute-start | bytes 12296 | tf_op jit(solution)/shard_map/ppermute | solution.py:87
  141.5 5.7 %collective-permute-start.12 = (f32[1024]{0:T(1024)S(1)}, f32[1024]{0:T(1024)S(1)}, u32[]{:S(2)}, u32[]{:S(2)}) collective-permute-start(f32[1024]{0:T(1024)S(1)} %add.49), channel_id=1, source_target_pairs={{32,0},{39,1},{2,32},{1,33},{34,2},{33,3},{4,34},{3,35},{36,4},{35... | collective-permute-start | bytes 12296 | tf_op jit(solution)/shard_map/ppermute | solution.py:87
  144.4 8.7 %collective-permute-start.13 = (f32[1024]{0:T(1024)S(1)}, f32[1024]{0:T(1024)S(1)}, u32[]{:S(2)}, u32[]{:S(2)}) collective-permute-start(f32[1024]{0:T(1024)S(1)} %get-tuple-element.17), channel_id=1, source_target_pairs={{38,1},{3,32},{32,3},{5,34},{34,5},{7,36},{36,7},{9,38},{46,9},{11... | collective-permute-start | bytes 12296 | tf_op jit(solution)/shard_map/ppermute | solution.py:87

commit v2 on v1

--- a/solution.py
+++ b/solution.py
@@ -28,19 +28,19 @@
 def hop_two(x, y, z, c):
     if c:
         t = (z + 1) % NZ
-        return (x, y - (t in (3, 5)) + (t == 0), t, c)
+        return (x, y - (t in (3, 5)), t, c)
     t = (z - 1) % NZ
-    return (x, y + (t in (0, 2, 4)), t, c)
+    return (x, y + (t in (2, 4)), t, c)
 
 
 def hop_three(x, y, z, c):
-    return (x, y, z - 1, c) if c else (x, y + (z in (6, 7)), z + 1, c)
+    return (x, y - (z == 1), z - 1, c) if c else (x, y + (z == 6), z + 1, c)
 
 
 def own_across(x, y, z, c):
     if not is_first(x, y, z, c):
         return (x, y, z, 1 - c)
-    return (x, y + 1, z, 0) if c else (x, y - (z in (1, 3, 5)), z, 1)
+    return (x, y + (z in (2, 4, 6)), z, 0) if c else (x, y - (z in (1, 3, 5)), z, 1)
 
 
 def own_along_x(x, y, z, c):
@@ -104,22 +104,23 @@
     return jnp.sum(block, axis=1), jnp.sum(block, axis=0)
 
 
+def after(value, *others):
+    return lax.optimization_barrier((value, *others))[0]
+
+
 def body(own):
     rows = own.shape[0]
+    half = rows // 2
     first = lax.axis_index("gx") % 2 != lax.axis_index("gy") % 2
 
     def pick(a, b):
         return jnp.where(first, a, b)
 
-    one = move(own, route(hop_one))
+    own_a, own_b = own[:half], own[half:]
+    one_a = move(own_a, route(hop_one))
+    one_b = move(own_b, route(hop_one))
     across = move(own, route(own_across))
     along = move(own, route(own_along_x))
-    own_late, _ = lax.optimization_barrier((own, one))
-    two = move(one, route(hop_two))
-    three = move(own_late, route(hop_three))
-    two_c = move(two, route(two_across))
-    two_x = move(two, route(two_along_x))
-    three_c = move(three, route(three_across))
 
     own_half = half_norms(own)
     diagonal = lax.broadcasted_iota(jnp.int32, (rows, rows), 0) == lax.broadcasted_iota(
@@ -127,20 +128,47 @@
     )
     same = jnp.where(diagonal, jnp.float32(0.0), kernel_block(own, own_half, own, own_half))
     total = jnp.sum(same, axis=1)
+    two_a = move(one_a, route(hop_two))
+    two_b = move(after(one_b, across, along, total), route(hop_two))
 
+    three_a = move(after(own_a, two_a), route(hop_three))
+    two_c_a = move(two_a, route(two_across))
+    two_x_a = move(two_a, route(two_along_x))
+    three_b = move(after(own_b, two_b), route(hop_three))
+    two_c_b = move(after(two_b, two_c_a), route(two_across))
+    two_x_b = move(after(two_b, two_x_a), route(two_along_x))
+
+    one = jnp.concatenate([one_a, one_b])
+    two = jnp.concatenate([two_a, two_b])
     two_half = half_norms(two)
     b_left, b_right = sums(
         across, half_norms(across), pick(own, two), pick(own_half, two_half)
     )
-    c_block, c_other = pick(along, two_c), pick(one, two)
+    c_block = pick(along, jnp.concatenate([two_c_a, two_c_b]))
+    c_other = pick(one, two)
     c_left, c_right = sums(c_block, half_norms(c_block), c_other, half_norms(c_other))
-    three_half = half_norms(three)
-    d_left, d_right = sums(three, three_half, two, two_half)
-    e_block = pick(three_c, two_x)
-    e_left, e_right = sums(e_block, half_norms(e_block), three, three_half)
+    three_a_half = half_norms(three_a)
+    three_c_a = move(three_a, route(three_across))
+    d_left_a, d_right_a = sums(three_a, three_a_half, two, two_half)
+    e_a = pick(three_c_a, two_x_a)
+    e_a_half = half_norms(e_a)
+    e_left_a, e_right_a = sums(e_a, e_a_half, three_a, three_a_half)
+
+    three_b, two, e_a, _ = lax.optimization_barrier(
+        (three_b, two, e_a, (b_left, c_left, d_left_a, e_left_a))
+    )
+    three_c_b = move(three_b, route(three_across))
+    three_b_half = half_norms(three_b)
+    d_left_b, d_right_b = sums(three_b, three_b_half, two, two_half)
+    e_left_c, e_right_b = sums(e_a, e_a_half, three_b, three_b_half)
+    three = jnp.concatenate([three_a, three_b])
+    three_half = jnp.concatenate([three_a_half, three_b_half])
+    e_b = pick(three_c_b, two_x_b)
+    e_left_b, e_right = sums(e_b, half_norms(e_b), three, three_half)
 
     zero = jnp.zeros_like(total)
     total = total + pick(b_right, zero)
+    b_left, c_left, _ = lax.optimization_barrier((b_left, c_left, (two_c_b, two_x_b)))
     total = total + move(b_left, back(route(own_across)))
     total = total + move(c_left, back(route(own_along_x)))
     one_pairs = [p for p in route(hop_one) if is_first(*PLACE[p[1]])]
@@ -148,11 +176,15 @@
         pick(c_right, c_left), back(one_pairs + route(hop_one, hop_two, two_across))
     )
     total = total + move(
-        d_right + pick(zero, b_right + c_right), back(route(hop_one, hop_two))
+        d_right_a + d_right_b + pick(zero, b_right + c_right), back(route(hop_one, hop_two))
     )
-    total = total + move(d_left + e_right, back(route(hop_three)))
     total = total + move(
-        e_left, back(route(hop_three, three_across) + route(hop_one, hop_two, two_along_x))
+        jnp.concatenate([d_left_a + e_right_a, d_left_b + e_right_b]) + e_right,
+        back(route(hop_three)),
+    )
+    total = total + move(
+        jnp.concatenate([e_left_a + e_left_c, e_left_b]),
+        back(route(hop_three, three_across) + route(hop_one, hop_two, two_along_x)),
     )
     return own_half + jnp.log(total)
 

time: 154 us -> 127 us (0.82)
  the two profiles are of different devices: /device:TPU:6 before, /device:TPU:33 now
where the time goes in v2:
time: 127 us; the launch traced here: 126 us
  starting transfers between devices  54.5 us (43%)
  waiting for transfers between devices  35.7 us (28%)
  matrix products  20.4 us (16%)
  other arithmetic  8.69 us (7%)
  local copies, waits for them, and re-layouts  6.87 us (5%)
    ppermute x20, starting transfers between devices, move(): return lax.ppermute(value, AXES, pairs)  54.5 us
    ppermute x20, waiting for transfers between devices, move(): return lax.ppermute(value, AXES, pairs)  35.7 us
    dot_general x8, matrix products, kernel_block(): lax.dot_general(left, right, (((1,), (1,)), ((), ())), preferred_element_...  20.4 us
    reduce_sum x8, other arithmetic, half_norms(): return jnp.sum(values * values, axis=1) / (2.0 * BAND)  7.99 us
    slice x1, local copies, waits for them, and re-layouts, body(): own_a, own_b = (own[:half], own[half:])  2.88 us
    unnamed x15, local copies, waits for them, and re-layouts  2.7 us
  transfers between devices with their start and end apart: 20, of which 8 were waited for; matrix products, arithmetic and copies ran while one was open for 25% of the time, Pallas kernels for 0%

profile of v2, /device:TPU:33, one launch (start us, length us, event | category | flops | bytes accessed | tf_op | source)
XLA Modules:
  0.0 126.4 jit_solution(5116691146577444146)
XLA Ops:
  0.0 2.9 %fusion.27 = (bf16[512,1024]{1,0:T(8,128)(2,1)}, bf16[512,1024]{1,0:T(8,128)(2,1)S(1)}) fusion(bf16[1024,1024]{1,0:T(8,128)(2,1)} %param.1), kind=kLoop, calls=%fused_computation.67 | loop fusion | bytes 4194304 | tf_op jit(solution)/shard_map/slice | solution.py:119
  2.9 1.6 %collective-permute-start = (bf16[512,1024]{1,0:T(8,128)(2,1)}, bf16[512,1024]{1,0:T(8,128)(2,1)S(1)}, u32[]{:S(2)}, u32[]{:S(2)}) collective-permute-start(bf16[512,1024]{1,0:T(8,128)(2,1)} %get-tuple-element.20), channel_id=1, source_target_pairs={{0,38},{1,33},{32,0},{33,3},{2,32},{3,35},{34,2},{35,5},{4,34},{5,... | collective-permute-start | bytes 3145736 | tf_op jit(solution)/shard_map/ppermute | solution.py:87
  4.5 0.9 collective-permute-start.3
  5.4 0.8 collective-permute-start.4
  6.2 4.8 %collective-permute-start.2 = (bf16[512,1024]{1,0:T(8,128)(2,1)S(1)}, bf16[512,1024]{1,0:T(8,128)(2,1)}, u32[]{:S(2)}, u32[]{:S(2)}) collective-permute-start(bf16[512,1024]{1,0:T(8,128)(2,1)S(1)} %get-tuple-element.21), channel_id=1, source_target_pairs={{0,38},{1,33},{32,0},{33,3},{2,32},{3,35},{34,2},{35,5},{4,34},{5,... | collective-permute-start | bytes 3145736 | tf_op jit(solution)/shard_map/ppermute | solution.py:87
  10.9 6.1 %collective-permute-done = bf16[512,1024]{1,0:T(8,128)(2,1)S(1)} collective-permute-done((bf16[512,1024]{1,0:T(8,128)(2,1)}, bf16[512,1024]{1,0:T(8,128)(2,1)S(1)}, u32[]{:S(2)}, u32[]{:S(2)}) %collective-permute-start) | collective-permute-done | bytes 1048608 | tf_op jit(solution)/shard_map/ppermute | solution.py:87
  17.0 1.6 %collective-permute-start.1 = (bf16[512,1024]{1,0:T(8,128)(2,1)S(1)}, bf16[512,1024]{1,0:T(8,128)(2,1)}, u32[]{:S(2)}, u32[]{:S(2)}) collective-permute-start(bf16[512,1024]{1,0:T(8,128)(2,1)S(1)} %collective-permute-done), channel_id=1, source_target_pairs={{0,38},{1,33},{32,0},{33,3},{2,32},{3,59},{34,10},{35,5},{4,34},{5... | collective-permute-start | bytes 3145736 | tf_op jit(solution)/shard_map/ppermute | solution.py:87
  18.7 0.5 multiply_reduce_fusion.4
  19.2 2.7 %select_reduce_fusion = f32[1024]{0:T(1024)S(1)} fusion(bf16[1024,1024]{1,0:T(8,128)(2,1)S(1)} %copy-done, f32[1024]{0:T(1024)S(1)} %broadcast_multiply_fusion.4), kind=kOutput, calls=%fused_computation.6 | convolution fusion | flops 2153774080 | bytes 2105344 | tf_op jit(solution)/shard_map/dot_general | solution.py:96
  21.9 6.9 %collective-permute-done.2 = bf16[512,1024]{1,0:T(8,128)(2,1)} collective-permute-done((bf16[512,1024]{1,0:T(8,128)(2,1)S(1)}, bf16[512,1024]{1,0:T(8,128)(2,1)}, u32[]{:S(2)}, u32[]{:S(2)}) %collective-permute-start.2) | collective-permute-done | bytes 1048608 | tf_op jit(solution)/shard_map/ppermute | solution.py:87
  28.7 1.6 %collective-permute-done.3 = bf16[1024,1024]{1,0:T(8,128)(2,1)S(1)} collective-permute-done((bf16[1024,1024]{1,0:T(8,128)(2,1)S(1)}, bf16[1024,1024]{1,0:T(8,128)(2,1)S(1)}, u32[]{:S(2)}, u32[]{:S(2)}) %collective-permute-start.3) | collective-permute-done | bytes 2097184 | tf_op jit(solution)/shard_map/ppermute | solution.py:87
  30.4 1.4 %copy-done.1 = bf16[1024,1024]{1,0:T(8,128)(2,1)} copy-done((bf16[1024,1024]{1,0:T(8,128)(2,1)}, bf16[1024,1024]{1,0:T(8,128)(2,1)S(1)}, u32[]{:S(2)}) %copy-start.1) | copy-done | bytes 2097176
  31.8 3.4 %collective-permute-start.5 = (bf16[512,1024]{1,0:T(8,128)(2,1)}, bf16[512,1024]{1,0:T(8,128)(2,1)}, u32[]{:S(2)}, u32[]{:S(2)}) collective-permute-start(bf16[512,1024]{1,0:T(8,128)(2,1)} %collective-permute-done.2), channel_id=1, source_target_pairs={{0,38},{1,33},{32,0},{33,3},{2,32},{3,59},{34,10},{35,5},{4,34},{5... | collective-permute-start | bytes 3145736 | tf_op jit(solution)/shard_map/ppermute | solution.py:87
  35.2 4.8 %collective-permute-done.1 = bf16[512,1024]{1,0:T(8,128)(2,1)} collective-permute-done((bf16[512,1024]{1,0:T(8,128)(2,1)S(1)}, bf16[512,1024]{1,0:T(8,128)(2,1)}, u32[]{:S(2)}, u32[]{:S(2)}) %collective-permute-start.1) | collective-permute-done | bytes 1048608 | tf_op jit(solution)/shard_map/ppermute | solution.py:87
  40.0 1.3 %collective-permute-start.6 = (bf16[512,1024]{1,0:T(8,128)(2,1)}, bf16[512,1024]{1,0:T(8,128)(2,1)}, u32[]{:S(2)}, u32[]{:S(2)}) collective-permute-start(bf16[512,1024]{1,0:T(8,128)(2,1)} %collective-permute-done.1), channel_id=1, source_target_pairs={{1,8},{32,57},{3,10},{34,59},{5,12},{36,61},{7,14},{38,63},{9,16},... | collective-permute-start | bytes 3145736 | tf_op jit(solution)/shard_map/ppermute | solution.py:87
  41.3 8.1 %collective-permute-start.13 = (bf16[512,1024]{1,0:T(8,128)(2,1)}, bf16[512,1024]{1,0:T(8,128)(2,1)}, u32[]{:S(2)}, u32[]{:S(2)}) collective-permute-start(bf16[512,1024]{1,0:T(8,128)(2,1)} %get-tuple-element.20), channel_id=1, source_target_pairs={{0,32},{1,39},{32,2},{33,25},{2,34},{3,33},{34,4},{35,3},{4,36},{5... | collective-permute-start | bytes 3145736 | tf_op jit(solution)/shard_map/ppermute | solution.py:87
  49.4 3.2 %collective-permute-start.8 = (bf16[512,1024]{1,0:T(8,128)(2,1)}, bf16[512,1024]{1,0:T(8,128)(2,1)S(1)}, u32[]{:S(2)}, u32[]{:S(2)}) collective-permute-start(bf16[512,1024]{1,0:T(8,128)(2,1)} %collective-permute-done.1), channel_id=1, source_target_pairs={{0,216},{33,105},{2,218},{35,107},{4,220},{37,109},{6,222},{39,111... | collective-permute-start | bytes 3145736 | tf_op jit(solution)/shard_map/ppermute | solution.py:87
  52.6 1.3 %constant_dynamic-update-slice_fusion.1 = bf16[1024,1024]{1,0:T(8,128)(2,1)S(1)} fusion(bf16[512,1024]{1,0:T(8,128)(2,1)} %collective-permute-done.1), kind=kLoop, calls=%fused_computation.45 | loop fusion | bytes 2097152
  53.9 0.5 multiply_reduce_fusion.3
  54.4 2.8 %collective-permute-done.5 = bf16[512,1024]{1,0:T(8,128)(2,1)} collective-permute-done((bf16[512,1024]{1,0:T(8,128)(2,1)}, bf16[512,1024]{1,0:T(8,128)(2,1)}, u32[]{:S(2)}, u32[]{:S(2)}) %collective-permute-start.5) | collective-permute-done | bytes 1048608 | tf_op jit(solution)/shard_map/ppermute | solution.py:87
  57.2 3.3 %collective-permute-start.14 = (bf16[512,1024]{1,0:T(8,128)(2,1)S(1)}, bf16[512,1024]{1,0:T(8,128)(2,1)S(1)}, u32[]{:S(2)}, u32[]{:S(2)}) collective-permute-start(bf16[512,1024]{1,0:T(8,128)(2,1)S(1)} %copy-done.6), channel_id=1, source_target_pairs={{0,32},{1,39},{32,2},{33,25},{2,34},{3,33},{34,4},{35,3},{4,36},{5... | collective-permute-start | bytes 3145736 | tf_op jit(solution)/shard_map/ppermute | solution.py:87
  60.5 1.3 %collective-permute-start.7 = (bf16[512,1024]{1,0:T(8,128)(2,1)}, bf16[512,1024]{1,0:T(8,128)(2,1)S(1)}, u32[]{:S(2)}, u32[]{:S(2)}) collective-permute-start(bf16[512,1024]{1,0:T(8,128)(2,1)} %collective-permute-done.5), channel_id=1, source_target_pairs={{1,8},{32,57},{3,10},{34,59},{5,12},{36,61},{7,14},{38,63},{9,16},... | collective-permute-start | bytes 3145736 | tf_op jit(solution)/shard_map/ppermute | solution.py:87
  61.8 1.3 %constant_dynamic-update-slice_fusion = bf16[1024,1024]{1,0:T(8,128)(2,1)S(1)} fusion(bf16[1024,1024]{1,0:T(8,128)(2,1)S(1)} %constant_dynamic-update-slice_fusion.1, bf16[512,1024]{1,0:T(8,128)(2,1)} %collective-permute-done.5), kind=kLoop, calls=%fused_computation.44 | loop fusion | bytes 2097152 | tf_op jit(solution)/shard_map/concatenate | solution.py:142
  63.1 8.9 %collective-permute-done.13 = bf16[512,1024]{1,0:T(8,128)(2,1)} collective-permute-done((bf16[512,1024]{1,0:T(8,128)(2,1)}, bf16[512,1024]{1,0:T(8,128)(2,1)}, u32[]{:S(2)}, u32[]{:S(2)}) %collective-permute-start.13) | collective-permute-done | bytes 1048608 | tf_op jit(solution)/shard_map/ppermute | solution.py:87
  72.0 1.5 %multiply_reduce_fusion.8 = f32[512]{0:T(512)S(1)} fusion(bf16[512,1024]{1,0:T(8,128)(2,1)} %collective-permute-done.13), kind=kLoop, calls=%fused_computation.25 | loop fusion | flops 1572352 | bytes 1050624 | tf_op jit(solution)/shard_map/reduce_sum | solution.py:92
  73.5 2.4 %multiply_reduce_fusion = (f32[1024]{0:T(1024)S(1)}, f32[1024]{0:T(1024)S(1)}) fusion(bf16[1024,1024]{1,0:T(8,128)(2,1)S(1)} %constant_dynamic-update-slice_fusion, bf16[512,1024]{1,0:T(8,128)(2,1)} %collective-permute-done.2, bf16[512,1024]{1,0:T(8,128)(2,1)S(1)} %collective-permute-done, pred[]{:T(512)S(6)} %ne.15), kind=kLoop, calls=%fused_computation.1 | loop fusion | flops 11532288 | bytes 4202497 | tf_op jit(solution)/shard_map/reduce_sum | solution.py:92
  76.0 2.1 %collective-permute-start.9 = (bf16[512,1024]{1,0:T(8,128)(2,1)}, bf16[512,1024]{1,0:T(8,128)(2,1)S(1)}, u32[]{:S(2)}, u32[]{:S(2)}) collective-permute-start(bf16[512,1024]{1,0:T(8,128)(2,1)} %collective-permute-done.5), channel_id=1, source_target_pairs={{0,216},{33,105},{2,218},{35,107},{4,220},{37,109},{6,222},{39,111... | collective-permute-start | bytes 3145736 | tf_op jit(solution)/shard_map/ppermute | solution.py:87
  78.1 1.5 %collective-permute-start.15 = (bf16[512,1024]{1,0:T(8,128)(2,1)}, bf16[512,1024]{1,0:T(8,128)(2,1)S(1)}, u32[]{:S(2)}, u32[]{:S(2)}) collective-permute-start(bf16[512,1024]{1,0:T(8,128)(2,1)} %collective-permute-done.13), channel_id=1, source_target_pairs={{0,1},{33,32},{2,3},{35,34},{4,5},{37,36},{6,7},{39,38},{8,9},{41,... | collective-permute-start | bytes 3145736 | tf_op jit(solution)/shard_map/ppermute | solution.py:87
  79.6 2.8 %fusion.12 = (f32[1024]{0:T(1024)S(1)}, f32[512]{0:T(512)S(1)}) fusion(f32[1024]{0:T(1024)S(1)} %get-tuple-element.47, f32[512]{0:T(512)S(1)} %broadcast_multiply_fusion.8, bf16[512,1024]{1,0:T(8,128)(2,1)} %collective-permute-done.13, bf16[1024,1024]{1,0:T(8,128)(2,1)S(1)} %constant_dynamic-update-slice_fusion), kind=kOutput, calls=%fused_computation.30 | convolution fusion | flops 1076361728 | bytes 3158016 | tf_op jit(solution)/shard_map/dot_general | solution.py:96
  82.5 2.9 %fusion.1 = (f32[1024]{0:T(1024)S(1)}, f32[1024]{0:T(1024)S(1)}) fusion(f32[1024]{0:T(1024)S(1)} %get-tuple-element.48, f32[1024]{0:T(1024)S(1)} %broadcast_multiply_fusion.3, bf16[1024,1024]{1,0:T(8,128)(2,1)S(1)} %copy-done.4, bf16[1024,1024]{1,0:T(8,128)(2,1)S(1)} %copy-done, bf16[1024,1024]{1,0:T(8,128)(2,1)S(1)} %constant_dynamic-update-slice_fusion, ...), kind=kOutput, calls=%fused_computation.10 | convolution fusion | flops 2153773056 | bytes 6307841 | tf_op jit(solution)/shard_map/dot_general | solution.py:96
  85.4 2.0 %multiply_reduce_fusion.1 = f32[1024]{0:T(1024)S(1)} fusion(bf16[1024,1024]{1,0:T(8,128)(2,1)S(1)} %copy-done.2, bf16[512,1024]{1,0:T(8,128)(2,1)S(1)} %collective-permute-done.7, bf16[512,1024]{1,0:T(8,128)(2,1)} %collective-permute-done.6, pred[]{:T(512)S(6)} %ne.15), kind=kLoop, calls=%fused_computation.2 | loop fusion | flops 8387584 | bytes 4198401 | tf_op jit(solution)/shard_map/reduce_sum | solution.py:92
  87.4 4.4 %fusion.2 = (f32[1024]{0:T(1024)S(1)}, f32[1024]{0:T(1024)S(1)}) fusion(f32[1024]{0:T(1024)S(1)} %broadcast_multiply_fusion, f32[1024]{0:T(1024)S(1)} %broadcast_multiply_fusion.1, bf16[1024,1024]{1,0:T(8,128)(2,1)S(1)} %constant_dynamic-update-slice_fusion, bf16[512,1024]{1,0:T(8,128)(2,1)} %collective-permute-done.2, ...), kind=kOutput, calls=%fused_computation.11 | convolution fusion | flops 2163210240 | bytes 8404993 | tf_op jit(solution)/shard_map/dot_general | solution.py:96
  91.8 0.4 multiply_reduce_fusion.7
  92.3 2.2 %fusion.25 = (f32[512]{0:T(512)S(1)}, f32[512]{0:T(512)S(1)}) fusion(f32[512]{0:T(512)S(1)} %broadcast_multiply_fusion.8, f32[512]{0:T(512)S(1)} %broadcast_multiply_fusion.7, bf16[512,1024]{1,0:T(8,128)(2,1)S(1)} %get-tuple-element.24, bf16[512,1024]{1,0:T(8,128)(2,1)} %collective-permute-done.13), kind=kOutput, calls=%fused_computation.65 | convolution fusion | flops 538180608 | bytes 2105344 | tf_op jit(solution)/shard_map/dot_general | solution.py:96
  94.5 1.4 %collective-permute-start.17 = (bf16[512,1024]{1,0:T(8,128)(2,1)S(1)}, bf16[512,1024]{1,0:T(8,128)(2,1)S(1)}, u32[]{:S(2)}, u32[]{:S(2)}) collective-permute-start(bf16[512,1024]{1,0:T(8,128)(2,1)S(1)} %collective-permute-done.14), channel_id=1, source_target_pairs={{0,1},{33,32},{2,3},{35,34},{4,5},{37,36},{6,7},{39,38},{8,9},{41,... | collective-permute-start | bytes 3145736 | tf_op jit(solution)/shard_map/ppermute | solution.py:87
  95.9 0.3 multiply_reduce_fusion.6
  96.1 0.9 fusion.26
  97.1 0.7 collective-permute-start.11
  97.8 1.6 %fusion.24 = (f32[1024]{0:T(1024)S(1)}, f32[512]{0:T(512)S(1)}) fusion(f32[1024]{0:T(1024)S(1)} %get-tuple-element.47, f32[512]{0:T(512)S(1)} %broadcast_multiply_fusion.6, bf16[512,1024]{1,0:T(8,128)(2,1)S(1)} %collective-permute-done.14, bf16[1024,1024]{1,0:T(8,128)(2,1)S(1)} %constant_dynamic-update-slice_fusion), kind=kOutput, calls=%fused_computation.64 | convolution fusion | flops 1076361728 | bytes 3158016 | tf_op jit(solution)/shard_map/dot_general | solution.py:96
  99.4 8.6 %collective-permute-start.16 = (f32[1024]{0:T(1024)S(1)}, f32[1024]{0:T(1024)S(1)}, u32[]{:S(2)}, u32[]{:S(2)}) collective-permute-start(f32[1024]{0:T(1024)S(1)} %get-tuple-element.46), channel_id=1, source_target_pairs={{6,0},{3,1},{38,32},{59,33},{0,2},{5,3},{32,34},{61,35},{10,4},{7,... | collective-permute-start | bytes 12296 | tf_op jit(solution)/shard_map/ppermute | solution.py:87
  107.9 1.8 %collective-permute-start.12 = (f32[1024]{0:T(1024)S(1)}, f32[1024]{0:T(1024)S(1)}, u32[]{:S(2)}, u32[]{:S(2)}) collective-permute-start(f32[1024]{0:T(1024)S(1)} %get-tuple-element.45), channel_id=1, source_target_pairs={{38,0},{3,33},{32,2},{5,35},{34,4},{7,37},{36,6},{1,39},{46,8},{11... | collective-permute-start | bytes 12296 | tf_op jit(solution)/shard_map/ppermute | solution.py:87
  109.8 0.4 multiply_reduce_fusion.5
  110.2 2.8 %fusion.14 = (f32[1024]{0:T(1024)S(1)}, f32[512]{0:T(512)S(1)}) fusion(f32[1024]{0:T(1024)S(1)} %pad_maximum_fusion, f32[512]{0:T(512)S(1)} %broadcast_multiply_fusion.5, bf16[512,1024]{1,0:T(8,128)(2,1)S(1)} %collective-permute-done.14, bf16[512,1024]{1,0:T(8,128)(2,1)} %collective-permute-done.13, bf16[512,1024]{1,0:T(8,128)(2,1)S(1)} %collective-permute-done.17, ...), kind=kOutput, calls=%fused_computation.32 | convolution fusion | flops 1081080320 | bytes 4206593 | tf_op jit(solution)/shard_map/dot_general | solution.py:96
  113.1 8.1 %collective-permute-start.19 = (f32[1024]{0:T(1024)S(1)}, f32[1024]{0:T(1024)S(1)}, u32[]{:S(2)}, u32[]{:S(2)}) collective-permute-start(f32[1024]{0:T(1024)S(1)} %pad_maximum_fusion.1), channel_id=1, source_target_pairs={{38,1},{3,32},{32,3},{5,34},{34,5},{7,36},{36,7},{1,38},{46,9},{11... | collective-permute-start | bytes 12296 | tf_op jit(solution)/shard_map/ppermute | solution.py:87
  121.2 0.1 collective-permute-start.18
  121.3 0.6 collective-permute-done.19
  121.9 3.9 %collective-permute-done.18 = f32[1024]{0:T(1024)S(1)} collective-permute-done((f32[1024]{0:T(1024)S(1)}, f32[1024]{0:T(1024)S(1)}, u32[]{:S(2)}, u32[]{:S(2)}) %collective-permute-start.18) | collective-permute-done | bytes 4128 | tf_op jit(solution)/shard_map/ppermute | solution.py:87
  125.8 0.6 log_add_fusion
  (42 shorter events, 0.2 us)
Async XLA Ops:
  0.0 4.5 %copy-start = (bf16[1024,1024]{1,0:T(8,128)(2,1)S(1)}, bf16[1024,1024]{1,0:T(8,128)(2,1)}, u32[]{:S(2)}) copy-start(bf16[1024,1024]{1,0:T(8,128)(2,1)} %param.1) | copy-start | bytes 6291460
  2.9 19.0 %copy-start.5 = (bf16[512,1024]{1,0:T(8,128)(2,1)}, bf16[512,1024]{1,0:T(8,128)(2,1)S(1)}, u32[]{:S(2)}) copy-start(bf16[512,1024]{1,0:T(8,128)(2,1)S(1)} %get-tuple-element.21) | copy-start | bytes 3145732
  2.9 14.2 %collective-permute-start = (bf16[512,1024]{1,0:T(8,128)(2,1)}, bf16[512,1024]{1,0:T(8,128)(2,1)S(1)}, u32[]{:S(2)}, u32[]{:S(2)}) collective-permute-start(bf16[512,1024]{1,0:T(8,128)(2,1)} %get-tuple-element.20), channel_id=1, source_target_pairs={{0,38},{1,33},{32,0},{33,3},{2,32},{3,35},{34,2},{35,5},{4,34},{5,... | collective-permute-start | bytes 3145736 | tf_op jit(solution)/shard_map/ppermute | solution.py:87
  4.5 25.9 %collective-permute-start.3 = (bf16[1024,1024]{1,0:T(8,128)(2,1)S(1)}, bf16[1024,1024]{1,0:T(8,128)(2,1)S(1)}, u32[]{:S(2)}, u32[]{:S(2)}) collective-permute-start(bf16[1024,1024]{1,0:T(8,128)(2,1)S(1)} %copy-done), channel_id=1, source_target_pairs={{0,1},{1,0},{32,57},{33,32},{2,3},{3,10},{34,59},{35,34},{4,5},{5,... | collective-permute-start | bytes 6291464 | tf_op jit(solution)/shard_map/ppermute | solution.py:87
  5.4 25.0 %collective-permute-start.4 = (bf16[1024,1024]{1,0:T(8,128)(2,1)S(1)}, bf16[1024,1024]{1,0:T(8,128)(2,1)S(1)}, u32[]{:S(2)}, u32[]{:S(2)}) collective-permute-start(bf16[1024,1024]{1,0:T(8,128)(2,1)S(1)} %copy-done), channel_id=1, source_target_pairs={{1,217},{32,96},{3,195},{34,98},{5,197},{36,100},{7,199},{38,110},... | collective-permute-start | bytes 6291464 | tf_op jit(solution)/shard_map/ppermute | solution.py:87
  6.2 22.6 %collective-permute-start.2 = (bf16[512,1024]{1,0:T(8,128)(2,1)S(1)}, bf16[512,1024]{1,0:T(8,128)(2,1)}, u32[]{:S(2)}, u32[]{:S(2)}) collective-permute-start(bf16[512,1024]{1,0:T(8,128)(2,1)S(1)} %get-tuple-element.21), channel_id=1, source_target_pairs={{0,38},{1,33},{32,0},{33,3},{2,32},{3,35},{34,2},{35,5},{4,34},{5,... | collective-permute-start | bytes 3145736 | tf_op jit(solution)/shard_map/ppermute | solution.py:87
  17.0 22.9 %collective-permute-start.1 = (bf16[512,1024]{1,0:T(8,128)(2,1)S(1)}, bf16[512,1024]{1,0:T(8,128)(2,1)}, u32[]{:S(2)}, u32[]{:S(2)}) collective-permute-start(bf16[512,1024]{1,0:T(8,128)(2,1)S(1)} %collective-permute-done), channel_id=1, source_target_pairs={{0,38},{1,33},{32,0},{33,3},{2,32},{3,59},{34,10},{35,5},{4,34},{5... | collective-permute-start | bytes 3145736 | tf_op jit(solution)/shard_map/ppermute | solution.py:87
  30.4 4.8 %copy-start.3 = (bf16[1024,1024]{1,0:T(8,128)(2,1)}, bf16[1024,1024]{1,0:T(8,128)(2,1)S(1)}, u32[]{:S(2)}) copy-start(bf16[1024,1024]{1,0:T(8,128)(2,1)S(1)} %collective-permute-done.3) | copy-start | bytes 6291460
  30.4 1.4 %copy-start.1 = (bf16[1024,1024]{1,0:T(8,128)(2,1)}, bf16[1024,1024]{1,0:T(8,128)(2,1)S(1)}, u32[]{:S(2)}) copy-start(bf16[1024,1024]{1,0:T(8,128)(2,1)S(1)} %collective-permute-done.4) | copy-start | bytes 6291460
  31.8 25.4 %collective-permute-start.5 = (bf16[512,1024]{1,0:T(8,128)(2,1)}, bf16[512,1024]{1,0:T(8,128)(2,1)}, u32[]{:S(2)}, u32[]{:S(2)}) collective-permute-start(bf16[512,1024]{1,0:T(8,128)(2,1)} %collective-permute-done.2), channel_id=1, source_target_pairs={{0,38},{1,33},{32,0},{33,3},{2,32},{3,59},{34,10},{35,5},{4,34},{5... | collective-permute-start | bytes 3145736 | tf_op jit(solution)/shard_map/ppermute | solution.py:87
  40.0 20.5 %collective-permute-start.6 = (bf16[512,1024]{1,0:T(8,128)(2,1)}, bf16[512,1024]{1,0:T(8,128)(2,1)}, u32[]{:S(2)}, u32[]{:S(2)}) collective-permute-start(bf16[512,1024]{1,0:T(8,128)(2,1)} %collective-permute-done.1), channel_id=1, source_target_pairs={{1,8},{32,57},{3,10},{34,59},{5,12},{36,61},{7,14},{38,63},{9,16},... | collective-permute-start | bytes 3145736 | tf_op jit(solution)/shard_map/ppermute | solution.py:87
  41.3 30.8 %collective-permute-start.13 = (bf16[512,1024]{1,0:T(8,128)(2,1)}, bf16[512,1024]{1,0:T(8,128)(2,1)}, u32[]{:S(2)}, u32[]{:S(2)}) collective-permute-start(bf16[512,1024]{1,0:T(8,128)(2,1)} %get-tuple-element.20), channel_id=1, source_target_pairs={{0,32},{1,39},{32,2},{33,25},{2,34},{3,33},{34,4},{35,3},{4,36},{5... | collective-permute-start | bytes 3145736 | tf_op jit(solution)/shard_map/ppermute | solution.py:87
  49.4 4.5 %copy-start.4 = (bf16[1024,1024]{1,0:T(8,128)(2,1)S(1)}, bf16[1024,1024]{1,0:T(8,128)(2,1)}, u32[]{:S(2)}) copy-start(bf16[1024,1024]{1,0:T(8,128)(2,1)} %copy-done.3) | copy-start | bytes 6291460
  49.4 7.8 %copy-start.6 = (bf16[512,1024]{1,0:T(8,128)(2,1)S(1)}, bf16[512,1024]{1,0:T(8,128)(2,1)}, u32[]{:S(2)}) copy-start(bf16[512,1024]{1,0:T(8,128)(2,1)} %copy-done.5) | copy-start | bytes 3145732
  49.4 26.6 %collective-permute-start.8 = (bf16[512,1024]{1,0:T(8,128)(2,1)}, bf16[512,1024]{1,0:T(8,128)(2,1)S(1)}, u32[]{:S(2)}, u32[]{:S(2)}) collective-permute-start(bf16[512,1024]{1,0:T(8,128)(2,1)} %collective-permute-done.1), channel_id=1, source_target_pairs={{0,216},{33,105},{2,218},{35,107},{4,220},{37,109},{6,222},{39,111... | collective-permute-start | bytes 3145736 | tf_op jit(solution)/shard_map/ppermute | solution.py:87
  57.2 37.3 %collective-permute-start.14 = (bf16[512,1024]{1,0:T(8,128)(2,1)S(1)}, bf16[512,1024]{1,0:T(8,128)(2,1)S(1)}, u32[]{:S(2)}, u32[]{:S(2)}) collective-permute-start(bf16[512,1024]{1,0:T(8,128)(2,1)S(1)} %copy-done.6), channel_id=1, source_target_pairs={{0,32},{1,39},{32,2},{33,25},{2,34},{3,33},{34,4},{35,3},{4,36},{5... | collective-permute-start | bytes 3145736 | tf_op jit(solution)/shard_map/ppermute | solution.py:87
  60.5 24.9 %collective-permute-start.7 = (bf16[512,1024]{1,0:T(8,128)(2,1)}, bf16[512,1024]{1,0:T(8,128)(2,1)S(1)}, u32[]{:S(2)}, u32[]{:S(2)}) collective-permute-start(bf16[512,1024]{1,0:T(8,128)(2,1)} %collective-permute-done.5), channel_id=1, source_target_pairs={{1,8},{32,57},{3,10},{34,59},{5,12},{36,61},{7,14},{38,63},{9,16},... | collective-permute-start | bytes 3145736 | tf_op jit(solution)/shard_map/ppermute | solution.py:87
  76.0 21.1 %collective-permute-start.9 = (bf16[512,1024]{1,0:T(8,128)(2,1)}, bf16[512,1024]{1,0:T(8,128)(2,1)S(1)}, u32[]{:S(2)}, u32[]{:S(2)}) collective-permute-start(bf16[512,1024]{1,0:T(8,128)(2,1)} %collective-permute-done.5), channel_id=1, source_target_pairs={{0,216},{33,105},{2,218},{35,107},{4,220},{37,109},{6,222},{39,111... | collective-permute-start | bytes 3145736 | tf_op jit(solution)/shard_map/ppermute | solution.py:87
  78.1 13.7 %collective-permute-start.15 = (bf16[512,1024]{1,0:T(8,128)(2,1)}, bf16[512,1024]{1,0:T(8,128)(2,1)S(1)}, u32[]{:S(2)}, u32[]{:S(2)}) collective-permute-start(bf16[512,1024]{1,0:T(8,128)(2,1)} %collective-permute-done.13), channel_id=1, source_target_pairs={{0,1},{33,32},{2,3},{35,34},{4,5},{37,36},{6,7},{39,38},{8,9},{41,... | collective-permute-start | bytes 3145736 | tf_op jit(solution)/shard_map/ppermute | solution.py:87
  82.5 2.9 %copy-start.2 = (bf16[1024,1024]{1,0:T(8,128)(2,1)S(1)}, bf16[1024,1024]{1,0:T(8,128)(2,1)}, u32[]{:S(2)}) copy-start(bf16[1024,1024]{1,0:T(8,128)(2,1)} %copy-done.1) | copy-start | bytes 6291460
  94.5 15.3 %collective-permute-start.17 = (bf16[512,1024]{1,0:T(8,128)(2,1)S(1)}, bf16[512,1024]{1,0:T(8,128)(2,1)S(1)}, u32[]{:S(2)}, u32[]{:S(2)}) collective-permute-start(bf16[512,1024]{1,0:T(8,128)(2,1)S(1)} %collective-permute-done.14), channel_id=1, source_target_pairs={{0,1},{33,32},{2,3},{35,34},{4,5},{37,36},{6,7},{39,38},{8,9},{41,... | collective-permute-start | bytes 3145736 | tf_op jit(solution)/shard_map/ppermute | solution.py:87
  97.1 24.2 %collective-permute-start.11 = (f32[1024]{0:T(1024)S(1)}, f32[1024]{0:T(1024)S(1)}, u32[]{:S(2)}, u32[]{:S(2)}) collective-permute-start(f32[1024]{0:T(1024)S(1)} %get-tuple-element.19), channel_id=1, source_target_pairs={{217,1},{96,32},{195,3},{98,34},{197,5},{100,36},{199,7},{110,38},... | collective-permute-start | bytes 12296 | tf_op jit(solution)/shard_map/ppermute | solution.py:87
  99.4 21.8 %collective-permute-start.16 = (f32[1024]{0:T(1024)S(1)}, f32[1024]{0:T(1024)S(1)}, u32[]{:S(2)}, u32[]{:S(2)}) collective-permute-start(f32[1024]{0:T(1024)S(1)} %get-tuple-element.46), channel_id=1, source_target_pairs={{6,0},{3,1},{38,32},{59,33},{0,2},{5,3},{32,34},{61,35},{10,4},{7,... | collective-permute-start | bytes 12296 | tf_op jit(solution)/shard_map/ppermute | solution.py:87
  107.9 13.3 %collective-permute-start.12 = (f32[1024]{0:T(1024)S(1)}, f32[1024]{0:T(1024)S(1)}, u32[]{:S(2)}, u32[]{:S(2)}) collective-permute-start(f32[1024]{0:T(1024)S(1)} %get-tuple-element.45), channel_id=1, source_target_pairs={{38,0},{3,33},{32,2},{5,35},{34,4},{7,37},{36,6},{1,39},{46,8},{11... | collective-permute-start | bytes 12296 | tf_op jit(solution)/shard_map/ppermute | solution.py:87
  109.8 11.5 %collective-permute-start.10 = (f32[1024]{0:T(1024)S(1)}, f32[1024]{0:T(1024)S(1)}, u32[]{:S(2)}, u32[]{:S(2)}) collective-permute-start(f32[1024]{0:T(1024)S(1)} %get-tuple-element.18), channel_id=1, source_target_pairs={{1,0},{0,1},{57,32},{32,33},{3,2},{10,3},{59,34},{34,35},{5,4},{12... | collective-permute-start | bytes 12296 | tf_op jit(solution)/shard_map/ppermute | solution.py:87
  113.1 8.8 %collective-permute-start.19 = (f32[1024]{0:T(1024)S(1)}, f32[1024]{0:T(1024)S(1)}, u32[]{:S(2)}, u32[]{:S(2)}) collective-permute-start(f32[1024]{0:T(1024)S(1)} %pad_maximum_fusion.1), channel_id=1, source_target_pairs={{38,1},{3,32},{32,3},{5,34},{34,5},{7,36},{36,7},{1,38},{46,9},{11... | collective-permute-start | bytes 12296 | tf_op jit(solution)/shard_map/ppermute | solution.py:87
  121.2 4.6 %collective-permute-start.18 = (f32[1024]{0:T(1024)S(1)}, f32[1024]{0:T(1024)S(1)}, u32[]{:S(2)}, u32[]{:S(2)}) collective-permute-start(f32[1024]{0:T(1024)S(1)} %maximum_add_fusion), channel_id=1, source_target_pairs={{32,0},{39,1},{2,32},{25,33},{34,2},{33,3},{4,34},{3,35},{36,4},{3... | collective-permute-start | bytes 12296 | tf_op jit(solution)/shard_map/ppermute | solution.py:87
